TPU v7x, 32 devices: a whole 2x2x4 slice. The times are simulated.
32 devices in a mesh: img: 4 (over y, x), row: 8 (over z, core).
Axes of the slice: x: 2, y: 2, z: 4, core: 2. Of those that a mesh axis runs over, the one named last changes fastest.
Arguments:
- kspace: float32 [2, 4, 16, 2, 320, 320], P(None, 'img', None, None, 'row'), may hold values from -6 to 6
- coil_maps: float32 [2, 4, 16, 2, 320, 320], P(None, 'img', None, None, 'row'), may hold values from -1.5 to 1.5
- target: float32 [2, 4, 2, 320, 320], P(None, 'img', None, 'row'), may hold values from -6 to 6
- row_mask: int32 [2, 4, 320], P(None, 'img'), may hold values from 0 to 1, as said below
- foreground: int32 [2, 4, 320, 320], P(None, 'img', 'row'), may hold values from 0 to 1
- anatomy: int32 [2, 4], P(None, 'img'), may hold values from 0 to 1
- first_weight: float32 [9, 64, 2], replicated, may hold values from -1.5 to 1.5
- middle_weight: float32 [3, 9, 64, 64], replicated, may hold values from -0.25 to 0.25
- last_weight: float32 [9, 2, 64], replicated, may hold values from -0.25 to 0.25
- norm_gains: float32 [4, 64], replicated, may hold values from 0.5 to 1.5
- norm_shifts: float32 [4, 64], replicated, may hold values from -1.5 to 1.5
- extra_params: float32 [3], replicated, may hold values from -1.5 to 1.5
- first_mean: float32 [9, 64, 2], replicated, may hold values from -0.0048828125 to 0.0048828125
- first_square: float32 [9, 64, 2], replicated, may hold values from 1.0986328e-08 to 4.3945313e-08
- middle_mean: float32 [3, 9, 64, 64], replicated, may hold values from -0.0048828125 to 0.0048828125
- middle_square: float32 [3, 9, 64, 64], replicated, may hold values from 1.0986328e-08 to 4.3945313e-08
- last_mean: float32 [9, 2, 64], replicated, may hold values from -0.0048828125 to 0.0048828125
- last_square: float32 [9, 2, 64], replicated, may hold values from 1.0986328e-08 to 4.3945313e-08
- gains_mean: float32 [4, 64], replicated, may hold values from -0.0048828125 to 0.0048828125
- gains_square: float32 [4, 64], replicated, may hold values from 1.0986328e-08 to 4.3945313e-08
- shifts_mean: float32 [4, 64], replicated, may hold values from -0.0048828125 to 0.0048828125
- shifts_square: float32 [4, 64], replicated, may hold values from 1.0986328e-08 to 4.3945313e-08
- extra_mean: float32 [3], replicated, may hold values from -0.046875 to 0.046875
- extra_square: float32 [3], replicated, may hold values from 1.0986328e-06 to 4.394531e-06
Outputs:
- first_updated: float32 [9, 64, 2], replicated
- first_average: float32 [9, 64, 2], replicated
- first_energy: float32 [9, 64, 2], replicated
- first_copy: bfloat16 [9, 64, 2], replicated
- middle_updated: float32 [3, 9, 64, 64], replicated
- middle_average: float32 [3, 9, 64, 64], replicated
- middle_energy: float32 [3, 9, 64, 64], replicated
- middle_copy: bfloat16 [3, 9, 64, 64], replicated
- last_updated: float32 [9, 2, 64], replicated
- last_average: float32 [9, 2, 64], replicated
- last_energy: float32 [9, 2, 64], replicated
- last_copy: bfloat16 [9, 2, 64], replicated
- gains_updated: float32 [4, 64], replicated
- gains_average: float32 [4, 64], replicated
- gains_energy: float32 [4, 64], replicated
- shifts_updated: float32 [4, 64], replicated
- shifts_average: float32 [4, 64], replicated
- shifts_energy: float32 [4, 64], replicated
- extra_updated: float32 [3], replicated
- extra_average: float32 [3], replicated
- extra_energy: float32 [3], replicated
- loss_total: float32 [], replicated
- pixel_count: int32 [], replicated
Inputs may be any that keep to these rules, and one draw needn't show every extreme that they name: `row_mask`: 1 on every row with |row - 160| < 20.
All inputs are finite; a program needn't handle non-finite values.
Results may differ from a plain program's by a relative error of at most 0.004.
The roundings to bfloat16 on the way count: a program that leaves them out, or rounds other values in their place, can miss the bound.
Values may be sent and summed in bfloat16 or wider, within the bound.
A program may use at most 320 MiB of HBM per device.

v0:
```python
import functools

import jax
import jax.numpy as jnp
import numpy as np
from jax import lax
from jax.experimental import pallas as pl
from jax.experimental.pallas import tpu as pltpu
from jax.sharding import PartitionSpec as P

COILS = 16
BRAIN_COILS = 12
UNROLLS = 1
CG_STEPS = 2
STEP = 10


PRECISE = lax.Precision.HIGHEST
EPS_NORM = 1e-05
BETA_ONE = 0.9
BETA_TWO = 0.999
ADAM_EPS = 1e-08
DECAY_RATE = 0.01
LEARN_RATES = (0.3, 0.05, 0.05, 0.4, 0.4, 0.4)


def with_halo(cells, sides, width):
    for axis, dim in sides:
        count = lax.axis_size(axis)
        ends = count - 1
        head = lax.slice_in_dim(cells, 0, width, axis=dim)
        tail = lax.slice_in_dim(cells, cells.shape[dim] - width, cells.shape[dim], axis=dim)
        cells = jnp.concatenate(
            [
                lax.ppermute(tail, axis, [(i, (i + 1) % count) for i in range(ends)]),
                cells,
                lax.ppermute(head, axis, [((i + 1) % count, i) for i in range(ends)]),
            ],
            axis=dim,
        )
    return cells


def dft_table(length, direction):
    index = jnp.arange(length, dtype=jnp.int32)
    phase = (index[:, None] * index[None, :] % length).astype(jnp.float32) * (2.0 * jnp.pi / length)
    factor = 1.0 / jnp.sqrt(jnp.float32(length))
    cosine = jnp.cos(phase) * factor
    sine = jnp.sin(phase) * factor * direction
    return jnp.stack([jnp.stack([cosine, -sine], 1), jnp.stack([sine, cosine], 1)], 0)


def along_width(field, table):
    return jnp.einsum("bcprw,pwqk->bcqrk", field, table, precision=PRECISE)


def along_height(field, table):
    return jnp.einsum("bcprw,prqk->bcqkw", field, table, precision=PRECISE)


def expand(image, maps):
    real_part, imag_part = (image[:, None, 0], image[:, None, 1])
    maps_re, maps_im = (maps[:, :, 0], maps[:, :, 1])
    return jnp.stack(
        [maps_re * real_part - maps_im * imag_part, maps_re * imag_part + maps_im * real_part], 2
    )


def combine(field, maps):
    field_re, field_im = (field[:, :, 0], field[:, :, 1])
    maps_re, maps_im = (maps[:, :, 0], maps[:, :, 1])
    return jnp.stack(
        [
            jnp.sum(maps_re * field_re + maps_im * field_im, 1),
            jnp.sum(maps_re * field_im - maps_im * field_re, 1),
        ],
        1,
    )


def to_columns(field):
    return lax.all_to_all(
        field.astype(jnp.bfloat16), "row", split_axis=4, concat_axis=3, tiled=True
    ).astype(field.dtype)


def to_rows(field):
    return lax.all_to_all(
        field.astype(jnp.bfloat16), "row", split_axis=3, concat_axis=4, tiled=True
    ).astype(field.dtype)


def make_normal(maps, mask_rows, forward, inverse, measured):
    zero_filled = combine(to_rows(along_height(measured * mask_rows, inverse)), maps)

    def normal(image):
        spectrum = to_columns(along_width(expand(image, maps), forward))
        spectrum = along_height(spectrum, forward) * mask_rows
        spectrum = to_rows(along_height(spectrum, inverse))
        return combine(along_width(spectrum, inverse), maps)

    return (normal, zero_filled)


def inner(left, right):
    return jnp.sum(left * right, axis=(1, 2, 3))


def per_image(values):
    return values[:, None, None, None]


def row_sums(values):
    return lax.psum(values, "row")


def solve(rhs, penalty, normal):
    state = jnp.zeros_like(rhs)
    residue = rhs
    search = rhs
    norm_now = row_sums(inner(residue, residue))
    kept = []
    for iterate in range(CG_STEPS):
        mapped = normal(search) + penalty * search
        curvature = row_sums(inner(search, mapped))
        stepsize = norm_now / curvature
        state = state + per_image(stepsize) * search
        residue = residue - per_image(stepsize) * mapped
        norm_next = row_sums(inner(residue, residue))
        kept.append((search, mapped, residue, norm_now, norm_next, curvature))
        search = residue + per_image(norm_next / norm_now) * search
        norm_now = norm_next
    return (state, kept)


def solve_backward(state_grad, kept, rhs, denoised, penalty, normal):
    search_grad = jnp.zeros_like(rhs)
    residue_grad = jnp.zeros_like(rhs)
    norm_grad = jnp.zeros(rhs.shape[0], jnp.float32)
    penalty_part = jnp.float32(0.0)
    for iterate in reversed(range(CG_STEPS)):
        search, mapped, residue, norm_now, norm_next, curvature = kept[iterate]
        factor_grad, along_search, joint_mapped, residue_mapped = lax.psum(
            (
                inner(search_grad, search),
                inner(state_grad, search),
                inner(residue_grad + search_grad, mapped),
                inner(residue, mapped),
            ),
            "row",
        )
        stepsize = norm_now / curvature
        factor = norm_next / norm_now
        norm_total = norm_grad + factor_grad / norm_now
        residue_full = residue_grad + search_grad + per_image(2.0 * norm_total) * residue
        stepsize_grad = along_search - (joint_mapped + 2.0 * norm_total * residue_mapped)
        curvature_grad = -stepsize_grad * norm_now / (curvature * curvature)
        mapped_grad = -per_image(stepsize) * residue_full + per_image(curvature_grad) * search
        penalty_part = penalty_part + jnp.sum(mapped_grad * search)
        search_grad = (
            per_image(factor) * search_grad
            + per_image(stepsize) * state_grad
            + per_image(curvature_grad) * mapped
            + normal(mapped_grad)
            + penalty * mapped_grad
        )
        residue_grad = residue_full
        norm_grad = -factor_grad * norm_next / (norm_now * norm_now) + stepsize_grad / curvature
    rhs_grad = residue_grad + search_grad + per_image(2.0 * norm_grad) * rhs
    penalty_part = penalty_part + jnp.sum(rhs_grad * denoised)
    return (penalty * rhs_grad, penalty_part)


def conv_forward(activation, weight):
    height, breadth = (activation.shape[2], activation.shape[3])
    padded = with_halo(activation, (("row", 2),), 1)
    padded = jnp.pad(padded, ((0, 0), (0, 0), (0, 0), (1, 1)))
    summed = jnp.zeros((activation.shape[0], weight.shape[1], height, breadth), jnp.float32)
    for tap_index in range(9):
        window = padded[
            :, :, tap_index // 3 : tap_index // 3 + height, tap_index % 3 : tap_index % 3 + breadth
        ]
        summed = summed + jnp.einsum(
            "oi,birw->borw", weight[tap_index], window, preferred_element_type=jnp.float32
        )
    return (summed, padded)


def conv_backward(upstream, padded, weight, need_input):
    height, breadth = (upstream.shape[2], upstream.shape[3])
    weight_grad = jnp.stack(
        [
            jnp.einsum(
                "borw,birw->oi",
                upstream,
                padded[
                    :,
                    :,
                    tap_index // 3 : tap_index // 3 + height,
                    tap_index % 3 : tap_index % 3 + breadth,
                ],
                preferred_element_type=jnp.float32,
            )
            for tap_index in range(9)
        ]
    )
    if not need_input:
        return (weight_grad, None)
    widened = with_halo(upstream, (("row", 2),), 1)
    widened = jnp.pad(widened, ((0, 0), (0, 0), (0, 0), (1, 1)))
    summed = jnp.zeros((upstream.shape[0], weight.shape[2], height, breadth), jnp.float32)
    for tap_index in range(9):
        start_r = 2 - tap_index // 3
        start_c = 2 - tap_index % 3
        window = widened[:, :, start_r : start_r + height, start_c : start_c + breadth]
        summed = summed + jnp.einsum(
            "oi,borw->birw", weight[tap_index], window, preferred_element_type=jnp.float32
        )
    return (weight_grad, summed)


def norm_sums(values):
    return lax.psum(values, ("img", "row"))


def channel(values):
    return values[None, :, None, None]


def cnn_forward(image, weights, gains, shifts, offset, pixels):
    activation = image.astype(jnp.bfloat16)
    kept = []
    for layer_index in range(4):
        linear, padded = conv_forward(activation, weights[layer_index])
        average = norm_sums(jnp.sum(linear, axis=(0, 2, 3))) / pixels
        centred = linear - channel(average)
        spread = norm_sums(jnp.sum(centred * centred, axis=(0, 2, 3))) / pixels
        inv_std = lax.rsqrt(spread + EPS_NORM)
        normed = centred * channel(inv_std)
        shaped = channel(gains[layer_index]) * normed + channel(shifts[layer_index])
        activation = jax.nn.silu(shaped).astype(jnp.bfloat16)
        kept.append((padded, normed, shaped, inv_std))
    result, padded = conv_forward(activation, weights[4])
    kept.append(padded)
    return (image + result + channel(offset), kept)


def cnn_backward(denoised_grad, kept, weights, gains, pixels, need_input):
    offset_grad = jnp.sum(denoised_grad, axis=(0, 2, 3))
    weight_grads = [None] * 5
    gain_grads = [None] * 4
    shift_grads = [None] * 4
    weight_grads[4], upstream = conv_backward(
        denoised_grad.astype(jnp.bfloat16), kept[4], weights[4], True
    )
    for layer_index in (3, 2, 1, 0):
        padded, normed, shaped, inv_std = kept[layer_index]
        sigmoid_val = jax.nn.sigmoid(shaped)
        shaped_grad = upstream * sigmoid_val * (1.0 + shaped * (1.0 - sigmoid_val))
        shift_local = jnp.sum(shaped_grad, axis=(0, 2, 3))
        gain_local = jnp.sum(shaped_grad * normed, axis=(0, 2, 3))
        shift_total, gain_total = lax.psum((shift_local, gain_local), ("img", "row"))
        gain_vec = gains[layer_index]
        linear_grad = channel(inv_std) * (
            shaped_grad * channel(gain_vec)
            - channel(gain_vec * shift_total / pixels)
            - normed * channel(gain_vec * gain_total / pixels)
        )
        shift_grads[layer_index] = shift_local
        gain_grads[layer_index] = gain_local
        weight_grads[layer_index], upstream = conv_backward(
            linear_grad.astype(jnp.bfloat16),
            padded,
            weights[layer_index],
            layer_index > 0 or need_input,
        )
    image_grad = None
    return (image_grad, weight_grads, jnp.stack(gain_grads), jnp.stack(shift_grads), offset_grad)


def adamw(weight, gradient, moment_one, moment_two, rate):
    first_new = BETA_ONE * moment_one + (1.0 - BETA_ONE) * gradient
    second_new = BETA_TWO * moment_two + (1.0 - BETA_TWO) * gradient * gradient
    corrected = first_new / (1.0 - BETA_ONE**STEP)
    divisor = jnp.sqrt(second_new / (1.0 - BETA_TWO**STEP)) + ADAM_EPS
    updated = weight - rate * (corrected / divisor + DECAY_RATE * weight)
    return (updated, first_new, second_new)


def general_local(arrays):
    (
        kspace, coil_maps, target, row_mask, foreground, anatomy, first_weight, middle_weight, last_weight, norm_gains, norm_shifts, extra_params,
    ) = arrays
    length = kspace.shape[-1]
    forward = dft_table(length, 1.0)
    inverse = dft_table(length, -1.0)
    pixel_total = lax.psum(jnp.sum(foreground).astype(jnp.float32), ("img", "row"))
    inv_count = 1.0 / pixel_total
    middle_low = middle_weight.astype(jnp.bfloat16)
    conv_weights = [
        first_weight.astype(jnp.bfloat16),
        middle_low[0],
        middle_low[1],
        middle_low[2],
        last_weight.astype(jnp.bfloat16),
    ]
    penalty = jnp.exp(extra_params[2])
    offset = extra_params[:2]
    images_here = kspace.shape[1]
    pixels = images_here * kspace.shape[4] * length * lax.axis_size("img") * lax.axis_size("row")
    first_grad = jnp.zeros_like(first_weight)
    middle_grad = jnp.zeros_like(middle_weight)
    last_grad = jnp.zeros_like(last_weight)
    gains_grad = jnp.zeros_like(norm_gains)
    shifts_grad = jnp.zeros_like(norm_shifts)
    offset_grad = jnp.zeros((2,), jnp.float32)
    penalty_grad = jnp.float32(0.0)
    loss_part = jnp.float32(0.0)
    for microbatch in range(kspace.shape[0]):
        limit = jnp.where(anatomy[microbatch] == 0, BRAIN_COILS, COILS)
        coil_on = (jnp.arange(kspace.shape[2])[None, :] < limit[:, None]).astype(jnp.float32)
        maps = coil_maps[microbatch] * coil_on[:, :, None, None, None]
        mask_rows = row_mask[microbatch].astype(jnp.float32)[:, None, None, :, None]
        measured = to_columns(along_width(kspace[microbatch], inverse))
        normal, zero_filled = make_normal(maps, mask_rows, forward, inverse, measured)
        state = zero_filled
        unroll = 0
        denoised, cnn_kept = cnn_forward(
            state, conv_weights, norm_gains, norm_shifts, offset, pixels
        )
        rhs = zero_filled + penalty * denoised
        state, cg_kept = solve(rhs, penalty, normal)
        saved = [(cnn_kept, cg_kept, rhs, denoised)]
        fg_mask = foreground[microbatch].astype(jnp.float32)[:, None]
        difference = state - target[microbatch]
        loss_part = loss_part + jnp.sum(fg_mask * difference * difference)
        state_grad = inv_count * 2.0 * fg_mask * difference
        for unroll in reversed(range(UNROLLS)):
            cnn_kept, cg_kept, rhs, denoised = saved[unroll]
            denoised_grad, penalty_part = solve_backward(
                state_grad, cg_kept, rhs, denoised, penalty, normal
            )
            penalty_grad = penalty_grad + penalty_part
            state_grad, weight_grads, gain_part, shift_part, offset_part = cnn_backward(
                denoised_grad, cnn_kept, conv_weights, norm_gains, pixels, unroll > 0
            )
            first_grad = first_grad + weight_grads[0]
            middle_grad = middle_grad + jnp.stack(weight_grads[1:4])
            last_grad = last_grad + weight_grads[4]
            gains_grad = gains_grad + gain_part
            shifts_grad = shifts_grad + shift_part
            offset_grad = offset_grad + offset_part
    extra_grad = jnp.concatenate([offset_grad, (penalty * penalty_grad)[None]])
    totals = lax.psum(
        (first_grad, middle_grad, last_grad, gains_grad, shifts_grad, extra_grad, loss_part),
        ("img", "row"),
    )
    return totals, pixel_total


BF16 = jnp.bfloat16
F32 = jnp.float32
MESH = pl.DeviceIdType.MESH
TILE = 128
BLOCK = 8
BACK_REACH = 3
FIRST_REACH = 6
GROUP = 4
HOOK_PART = 4
REACH = 8
VMEM_BYTES = 58 * 1024 * 1024


def padded(length):
    return -(-length // TILE) * TILE


def fits(kspace, first_weight, mesh_rows):
    micro, images, coils, _, rows, length = kspace.shape
    channels = first_weight.shape[1]
    return (
        images == 1
        and micro == 2
        and 2 * channels == TILE
        and channels % 16 == 0
        and rows * mesh_rows == length
        and mesh_rows & (mesh_rows - 1) == 0
        and rows % BLOCK == 0
        and (2 * rows) % 16 == 0
        and (coils * rows) % TILE == 0
        and padded(length) > length
    )


def phases(length):
    index = np.arange(length)
    angle = 2.0 * np.pi * (np.outer(index, index) % length) / length
    return np.cos(angle) / np.sqrt(length), np.sin(angle) / np.sqrt(length)


def high_low(table):
    high = table.astype(BF16)
    low = (table - high.astype(F32)).astype(BF16)
    return high, low


def np_high_low(table):
    table = np.asarray(table, np.float32)
    high = table.astype(BF16)
    low = (table - high.astype(np.float32)).astype(BF16)
    return jnp.asarray(high), jnp.asarray(low)


def dot(left, right):
    return jnp.dot(left, right, preferred_element_type=F32)


def dot_nt(left, right):
    return lax.dot_general(left, right, (((1,), (1,)), ((), ())), preferred_element_type=F32)


def knock(peers):
    barrier = pltpu.get_barrier_semaphore()
    for peer in peers:
        pl.semaphore_signal(barrier, inc=1, device_id=peer, device_id_type=MESH)


def admit(peers):
    pl.semaphore_wait(pltpu.get_barrier_semaphore(), len(peers))


def partner(me, step):
    other, bit = 0, 1
    while bit <= step:
        own = lax.rem(lax.div(me, bit), 2)
        other = other + bit * (1 - own if step & bit else own)
        bit *= 2
    return other + lax.div(me, bit) * bit


def row_peers(rows):
    image, row = lax.axis_index("img"), lax.axis_index("row")
    steps = sorted(range(1, rows), key=lambda step: (-step.bit_length(), step))
    return [(image, partner(row, step)) for step in steps]


def image_peers(images):
    image, row = lax.axis_index("img"), lax.axis_index("row")
    return [(lax.rem(image + step, images), row) for step in range(1, images)]


def remote(source, target, send, receive, peer):
    return pltpu.make_async_remote_copy(
        src_ref=source,
        dst_ref=target,
        send_sem=send,
        recv_sem=receive,
        device_id=peer,
        device_id_type=MESH,
    )


def params(vmem=VMEM_BYTES, **kwargs):
    return pltpu.CompilerParams(vmem_limit_bytes=vmem, **kwargs)


def in_vmem():
    return pl.BlockSpec(memory_space=pltpu.VMEM)


def anywhere():
    return pl.BlockSpec(memory_space=pl.ANY)


def three_parts(values):
    high = values.astype(BF16)
    rest = values - high.astype(F32)
    middle = rest.astype(BF16)
    return high, middle, (rest - middle.astype(F32)).astype(BF16)


def join_lanes(pieces, wide):
    short = wide - sum(piece.shape[1] for piece in pieces)
    if short:
        pieces = pieces + [jnp.zeros((pieces[0].shape[0], short), pieces[0].dtype)]
    return jnp.concatenate(pieces, axis=1)


def join_rows(pieces, height):
    short = height - sum(piece.shape[0] for piece in pieces)
    if short:
        pieces = pieces + [jnp.zeros((short, pieces[0].shape[1]), pieces[0].dtype)]
    return jnp.concatenate(pieces, axis=0)


def start_exchange(
    sizes, meet, kspace, maps, target, foreground, row_mask, anatomy, first, middle, last, turn_high, turn_low, pick, cosine, sine,
    fourier_high, fourier_low,
    filled, maps_out, halo, planes, normal, first_table, middle_tables, last_table, middle_back, last_back, counted,
    fields, staged, spread, flat, landed, edges, loaded, send, receive, own, send_flat, receive_flat, send_edge, receive_edge,
):
    micro, coils, rows, length, parts = sizes
    wide = padded(length)
    image, me = lax.axis_index("img"), lax.axis_index("row")
    peers = row_peers(parts)
    slots = [(batch, kind) for batch in range(micro) for kind in (1, 0)]
    loads = {}

    def load_field(index):
        if index < len(slots):
            batch, kind = slots[index]
            for part in range(2):
                source = (kspace, maps)[kind].at[batch, :, part]
                loads[index, part] = pltpu.make_async_copy(source, fields.at[index % 2, part], loaded.at[index, part])
                loads[index, part].start()

    load_field(0)
    load_field(1)
    arrivals = [[] for _ in range(micro)]
    slabs = 2 * rows
    def send_slot(index):
        batch, kind = slots[index]
        total = None
        for part in range(2):
            loads[index, part].wait()
            field = fields[index % 2, part].reshape(coils * rows, length)
            if kind == 0:
                high, low = high_low(field)
                term = (
                    dot_nt(turn_high[part], high)
                    + dot_nt(turn_low[part], high)
                    + dot_nt(turn_high[part], low)
                )
            else:
                term = dot_nt(pick[part], field.astype(BF16))
            total = term if total is None else total + term
        slot = 2 * batch + kind
        staged[slot] = total.astype(BF16).reshape(parts, slabs, coils * rows)
        load_field(index + 2)
        if index == 0:
            meet()
        for step, peer in enumerate(peers):
            copy = remote(
                staged.at[slot, peer[1]], spread.at[slot, me], send.at[slot, step], receive.at[slot, step], peer
            )
            copy.start()
            arrivals[batch].append(copy)
        local = pltpu.make_async_copy(staged.at[slot, me], spread.at[slot, me], own.at[slot])
        local.start()
        arrivals[batch].append(local)

    for index in range(len(slots) - 1):
        send_slot(index)
    flats = exchange_planes(sizes, target, foreground, pick, counted, flat, landed, send_flat, receive_flat, me, peers)
    for batch in range(micro):
        chosen = join_lanes([row_mask[batch].astype(F32)], wide)
        cos_on, sin_on = cosine[...] * chosen, sine[...] * chosen

        def product(left, right):
            return jnp.dot(left, right, precision=PRECISE, preferred_element_type=F32)

        real = product(cos_on, cosine[...]) + product(sin_on, sine[...])
        imag = product(sin_on, cosine[...]) - product(cos_on, sine[...])
        diagonal = [lax.broadcasted_iota(jnp.int32, real.shape, axis) for axis in range(2)]
        real = jnp.where(diagonal[0] == diagonal[1], 0.0, real)
        for block, value in (((0, 0), real), ((0, 1), -imag), ((1, 0), imag), ((1, 1), real)):
            normal[batch, pl.ds(block[0] * wide, wide), pl.ds(block[1] * wide, wide)] = value.astype(BF16)
    put_tables(first, middle, last, first_table, middle_tables, last_table, middle_back, last_back)

    def arrive(batch):
        for copy in arrivals[batch]:
            copy.wait()
        knee = jnp.where(anatomy[0:1, batch : batch + 1] == 0, 0.0, 1.0)
        real, imag = zero_fill(
            (coils, rows, parts, wide),
            knee,
            spread.at[2 * batch],
            spread.at[2 * batch + 1],
            join_lanes([row_mask[batch].astype(F32)], wide),
            fourier_high,
            fourier_low,
            maps_out.at[batch],
        )
        put_pair(filled.at[batch], (real, imag))
        put_edges(edges.at[:, batch], real, imag)
        moved = image_halo(parts, batch, edges, halo, send_edge, receive_edge)
        for copy in moved:
            copy.start()
        if batch == 0:
            send_slot(len(slots) - 1)
            for copy in flats:
                copy.wait()
            for image_batch in range(micro):
                for plane in range(3):
                    at = (3 * image_batch + plane) * rows
                    pieces = [landed[block, :, at : at + rows] for block in range(parts)]
                    planes[image_batch, plane] = join_lanes(pieces, wide)
        for copy in moved:
            copy.wait()

    return arrive


def exchange_planes(
    sizes, target, foreground, pick, counted, flat, landed, send_flat, receive_flat, me, peers
):
    micro, _, rows, length, parts = sizes
    shown = [foreground[batch].astype(F32) for batch in range(micro)]
    count = functools.reduce(jnp.add, [jnp.sum(jnp.sum(s, axis=1, keepdims=True), axis=0, keepdims=True) for s in shown])
    counted[...] = jnp.broadcast_to(count, (1, TILE))
    stack = []
    for batch in range(micro):
        stack += [target[batch, 0], target[batch, 1], shown[batch]]
    stack = jnp.concatenate(stack, axis=0)
    plain = pick[0].reshape(parts, 2 * rows, length)[:, :rows].reshape(length, length)
    turned = functools.reduce(jnp.add, [dot_nt(plain, piece) for piece in three_parts(stack)])
    lanes = flat.shape[2]
    flat[...] = join_lanes([turned], lanes).reshape(parts, rows, lanes)
    landed[me] = flat[me]
    flats = []
    for step, peer in enumerate(peers):
        copy = remote(flat.at[peer[1]], landed.at[me], send_flat.at[step], receive_flat.at[step], peer)
        copy.start()
        flats.append(copy)
    return flats


def put_tables(first, middle, last, first_table, middle_tables, last_table, middle_back, last_back):
    taps = range(3)
    turned = [join_rows([first[tap]], 8).T[:, :2] for tap in range(9)]
    first_table[...] = jnp.concatenate(
        [join_lanes([turned[3 * kr + kw] for kr in taps], 16) for kw in taps], axis=0
    ).astype(BF16)
    last_table[...] = jnp.concatenate(
        [join_rows([jnp.concatenate([last[3 * kr + kw] for kr in taps], axis=1)], 8) for kw in taps], axis=0
    ).astype(BF16)
    turned = [join_rows([last[tap]], 8).T[:, :2] for tap in range(9)]
    last_back[...] = jnp.concatenate(
        [join_lanes([turned[3 * (2 - m) + 2 - n] for m in taps], 16) for n in taps], axis=0
    ).astype(BF16)
    for layer in range(3):
        weights = [middle[layer, tap] for tap in range(9)]
        turned = [weight.T for weight in weights]
        middle_tables[layer] = jnp.concatenate(
            [jnp.concatenate([weights[3 * kr + kw] for kr in taps], axis=1) for kw in taps], axis=0
        ).astype(BF16)
        middle_back[layer] = jnp.concatenate(
            [jnp.concatenate([turned[3 * (2 - m) + 2 - n] for m in taps], axis=1) for n in taps], axis=0
        ).astype(BF16)


def gather_lanes(blocks, coil, rows, wide):
    pieces = [block[:, coil * rows : (coil + 1) * rows] for block in blocks]
    height = pieces[0].shape[0]
    short = wide - rows * len(pieces)
    return jnp.concatenate(pieces + [jnp.zeros((height, short), pieces[0].dtype)], axis=1)


def zero_fill(sizes, knee, fields, senses, chosen, fourier_high, fourier_low, maps_out):
    coils, rows, parts, wide = sizes
    real = jnp.zeros((rows, wide), F32)
    imag = jnp.zeros((rows, wide), F32)
    chosen = chosen.astype(BF16)
    group = 4
    for first in range(0, coils, group):
        stack = []
        for coil in range(first, first + group):
            sense = gather_lanes([senses[s] for s in range(parts)], coil, rows, wide)
            maps_out[coil] = sense if coil < BRAIN_COILS else sense * knee.astype(BF16)
            stack.append(gather_lanes([fields[s] for s in range(parts)], coil, rows, wide) * chosen)
        stack = jnp.concatenate(stack, axis=0)
        turned = dot(stack, fourier_high[...]) + dot(stack, fourier_low[...])
        for place in range(group):
            top = 2 * rows * place
            upper, lower = turned[top : top + rows], turned[top + rows : top + 2 * rows]
            field_re = upper[:, :wide] - lower[:, wide:]
            field_im = upper[:, wide:] + lower[:, :wide]
            sense = maps_out[first + place].astype(F32)
            sense_re, sense_im = sense[:rows], sense[rows:]
            real = real + sense_re * field_re + sense_im * field_im
            imag = imag + sense_re * field_im - sense_im * field_re
    return real, imag


def put_edges(edges, real, imag):
    rows = real.shape[0]
    edges[0] = jnp.concatenate([real[:REACH], imag[:REACH]], axis=0)
    edges[1] = jnp.concatenate([real[rows - REACH :], imag[rows - REACH :]], axis=0)


def lane_row(columns):
    return jnp.sum(columns.T, axis=0, keepdims=True)


def spread_row(row):
    return jnp.broadcast_to(row, (TILE, row.shape[1])).T


def padded_rows(rows):
    return join_rows([join_lanes([row], TILE) for row in rows], 8)


def merge(sums, squares, count):
    total = functools.reduce(jnp.add, sums)
    mean = total / (count * len(sums))
    square = None
    for part, own in zip(sums, squares):
        shift = part / count - mean
        term = own + count * shift * shift
        square = term if square is None else square + term
    return total, square


def repeat_lanes(block, wide):
    return jnp.concatenate([block] * (wide // TILE), axis=1)


def lane_mask(length, wide):
    whole = length // TILE * TILE

    def clear(values):
        tail = values[:, whole:]
        keep = lax.broadcasted_iota(jnp.int32, tail.shape, 1) < length - whole
        return jnp.concatenate([values[:, :whole], jnp.where(keep, tail, 0.0)], axis=1)

    return clear


def fold(values):
    parts = [values[:, at : at + TILE] for at in range(0, values.shape[1], TILE)]
    return functools.reduce(jnp.add, parts)


def put_shifted(stack, values, at):
    channels, wide = values.shape
    stack[0:channels, at : at + wide] = pltpu.roll(values, 1, 1)
    stack[channels : 2 * channels, at : at + wide] = values
    stack[2 * channels : 3 * channels, at : at + wide] = pltpu.roll(values, wide - 1, 1)


def lane_at(column, wide):
    return pl.multiple_of(column * wide, TILE) if not isinstance(column, int) else column * wide


class Sums:
    def __init__(self, parts, images, refs):
        self.message, self.held, self.second, self.held_second, self.send, self.receive = refs
        self.rows, self.cols = row_peers(parts), image_peers(images)

    def copies(self, slot, stage):
        source, target = ((self.message, self.held), (self.second, self.held_second))[stage]
        peers = (self.rows, self.cols)[stage]
        base = stage * len(self.rows)
        return [
            remote(
                source.at[slot],
                target.at[slot + (index,)],
                self.send.at[slot + (base + index,)],
                self.receive.at[slot + (base + index,)],
                peer,
            )
            for index, peer in enumerate(peers)
        ]

    def start(self, slot, stage, values):
        (self.message, self.second)[stage][slot] = values
        for copy in self.copies(slot, stage):
            copy.start()

    def collect(self, slot, stage):
        blocks = [(self.message, self.second)[stage][slot]]
        for index, copy in enumerate(self.copies(slot, stage)):
            copy.wait_recv()
            blocks.append((self.held, self.held_second)[stage][slot + (index,)])
        return blocks

    def settle(self, slot, stages=(0, 1)):
        for stage in stages:
            for copy in self.copies(slot, stage):
                copy.wait_send()

    @staticmethod
    def scratch(slots, parts, images):
        return [
            pltpu.VMEM(slots + (8, TILE), F32),
            pltpu.VMEM(slots + (parts - 1, 8, TILE), F32),
            pltpu.VMEM(slots + (8, TILE), F32),
            pltpu.VMEM(slots + (max(images - 1, 1), 8, TILE), F32),
            pltpu.SemaphoreType.DMA(slots + (parts + images - 2,)),
            pltpu.SemaphoreType.DMA(slots + (parts + images - 2,)),
        ]


class Ends:
    def __init__(self, parts):
        me = lax.axis_index("row")
        self.left, self.right = me > 0, me < parts - 1

    def clear(self, values, column, width):
        if column < 0:
            return jnp.where(self.left, values, 0.0)
        if column >= width:
            return jnp.where(self.right, values, 0.0)
        return values


def ring_pass(table, take, fill, emit, out_rows, width, wide, hook):
    fill(0)
    fill(1)
    product = dot(table, take(0))
    older = product[0:out_rows, :wide] + product[out_rows : 2 * out_rows, wide:]
    newer = product[0:out_rows, wide:]
    last = width // 2
    for couple in range(1, last + 1):
        if hook is not None and couple == last * HOOK_PART // 8:
            hook()
        product = dot(table, take(couple))
        if couple < last:
            fill(couple + 1)
        for place in range(2):
            piece = product[:, place * wide : (place + 1) * wide]
            emit(2 * couple - 2 + place, older + piece[2 * out_rows : 3 * out_rows])
            older = newer + piece[out_rows : 2 * out_rows]
            newer = piece[0:out_rows]


def silu_half(values, scale, offset):
    half = values * scale + offset
    return half, jnp.tanh(half)


def put_image(image, halo, place, stack, ends, reach):
    _, width, wide = image.shape
    blocks = {-REACH: (halo[0, place, :REACH], halo[0, place, REACH:]), width: (halo[1, place, :REACH], halo[1, place, REACH:])}
    for first in range(0, width, 8):
        blocks[first] = (image[0, first : first + 8], image[1, first : first + 8])
    for first, (real, imag) in blocks.items():
        real, imag = ends.clear(real, first, width), ends.clear(imag, first, width)
        rolled = [pltpu.roll(real, 1, 1), pltpu.roll(imag, 1, 1), real, imag, pltpu.roll(real, wide - 1, 1), pltpu.roll(imag, wide - 1, 1)]
        for offset in range(8):
            at = first + offset + reach
            if 0 <= at < width + 2 * reach:
                rows = [block[offset : offset + 1] for block in rolled]
                stack[:, at * wide : (at + 1) * wide] = join_rows(rows, 16).astype(BF16)


def image_halo(parts, batch, edges, halo, send, receive):
    image, me = lax.axis_index("img"), lax.axis_index("row")
    left, right = lax.rem(me + parts - 1, parts), lax.rem(me + 1, parts)
    places = [((image, left), 0), ((image, right), 1)]
    return [
        remote(edges.at[side, batch], halo.at[1 - side, batch], send.at[batch, side], receive.at[batch, side], peer)
        for peer, side in places
    ]


def forward_kernel(
    sizes, kspace, maps, target, foreground, row_mask, anatomy, first, middle_weight, last, turn_high, turn_low, pick,
    cosine, sine, fourier_high, fourier_low, gains, shifts,
    filled, maps_out, planes, normal, middle_back, last_back, layers, coefs, rows_out, images_out, result,
    fields, staged, spread, flat, landed, edges, halo_image, first_table, middle_tables, last_table, counted,
    loaded, send, receive, own, send_flat, receive_flat, send_edge, receive_edge,
    lin, even, odd, pivot, total, square, *refs,
):
    micro, coils, rows, length, parts, images = sizes
    _, _, width, wide = filled.shape
    channels = lin.shape[3]
    count = width * length
    whole = length // TILE * TILE
    stacks = (even, odd)
    sums = Sums(parts, images, refs[:6])
    (saved,) = refs[6:]
    ends = Ends(parts)
    clear = lane_mask(length, wide)
    knock(sums.rows + sums.cols)
    arrive = start_exchange(
        (micro, coils, rows, length, parts), lambda: admit(sums.rows + sums.cols),
        kspace, maps, target, foreground, row_mask, anatomy, first, middle_weight, last, turn_high, turn_low, pick, cosine, sine,
        fourier_high, fourier_low,
        filled, maps_out, halo_image, planes, normal, first_table, middle_tables, last_table, middle_back, last_back, counted,
        fields, staged, spread, flat, landed, edges, loaded, send, receive, own, send_flat, receive_flat, send_edge, receive_edge,
    )

    def band(layer, batch):
        return lin.at[batch, lax.rem(layer, 2)]

    def save(layer, batch):
        kept = band(layer, batch).at[pl.ds(FIRST_REACH - BACK_REACH, width + 2 * BACK_REACH)]
        return pltpu.make_async_copy(kept, layers.at[layer, batch], saved.at[layer, batch])

    def begin(layer, batch, not_first):
        if not_first:
            save(layer - 1, batch).wait()
        moments = jnp.concatenate([total[...], square[...]], axis=0).T
        moments = jnp.sum(moments, axis=0, keepdims=True)
        delta = moments[:, :channels] / count
        spread = moments[:, channels:] - count * delta * delta
        centre = pivot[...].T[0:1]
        sums.start((layer, batch), 0, padded_rows([count * (centre + delta), spread, counted[:, :channels]]))
        save(layer, batch).start()

    def join(blocks, number):
        blocks = [block[:, :channels] for block in blocks]
        added, spread = merge([block[0:1] for block in blocks], [block[1:2] for block in blocks], number)
        return added, spread, functools.reduce(jnp.add, [block[2:3] for block in blocks])

    def middle(layer, batch):
        joined = join(sums.collect((layer, batch), 0), count)
        sums.start((layer, batch), 1, padded_rows(joined))

    def end(layer, batch):
        added, spread, plain = join(sums.collect((layer, batch), 1), count * parts)
        pixels = count * parts * images
        gain, shift = gains[pl.ds(layer, 1), :], shifts[pl.ds(layer, 1), :]
        inverse = lax.rsqrt(spread / pixels + EPS_NORM)
        offset = -(added / pixels) * inverse
        coefs[layer, batch, 0] = spread_row(0.5 * gain * inverse)
        coefs[layer, batch, 1] = spread_row(0.5 * (shift + gain * offset))
        coefs[layer, batch, 2] = spread_row(inverse)
        coefs[layer, batch, 3] = spread_row(offset)
        rows_out[layer, batch] = join_rows([gain, shift, inverse, offset, plain], 8)

    def keeper(out, reach):
        held = []

        def emit(column, value):
            column = column - reach
            out[FIRST_REACH + column] = value
            if not 0 <= column < width:
                return
            if column == 0:
                mean = jnp.sum(clear(value), axis=1, keepdims=True) / length
                pivot[...] = jnp.broadcast_to(mean, pivot.shape)
            if column % BLOCK == 0:
                held[:] = [jnp.zeros((channels, TILE), F32), jnp.zeros((channels, TILE), F32)]
            centre = pivot[...]
            for at in range(0, wide, TILE):
                shift = value[:, at : at + TILE] - centre
                if at >= whole:
                    lane = lax.broadcasted_iota(jnp.int32, shift.shape, 1)
                    shift = jnp.where(lane < length - at, shift, 0.0)
                held[0] = held[0] + shift
                held[1] = held[1] + shift * shift
            if column == BLOCK - 1:
                total[...], square[...] = held
            elif column % BLOCK == BLOCK - 1:
                total[...] += held[0]
                square[...] += held[1]

        return emit

    def first_layer(batch, hook):
        source = images_out.at[batch]
        put_image(filled.at[batch], halo_image, batch, source, ends, FIRST_REACH + 1)
        ring_pass(
            first_table[...],
            lambda couple: source[:, 2 * couple * wide : 2 * (couple + 1) * wide],
            lambda couple: None,
            keeper(band(0, batch), FIRST_REACH),
            channels,
            width + 2 * FIRST_REACH,
            wide,
            hook,
        )

    def inner_layer(layer, batch, table, out_rows, reach, emit, hook):
        source = band(layer, batch)
        scale, offset = repeat_lanes(coefs[layer, batch, 0], wide), repeat_lanes(coefs[layer, batch, 1], wide)

        def fill(couple):
            for place in range(2):
                column = 2 * couple + place - reach - 1
                half, curve = silu_half(source[FIRST_REACH + column], scale, offset)
                active = ends.clear(clear(half * curve + half), column, width)
                put_shifted(stacks[couple % 2], active.astype(BF16), place * wide)

        ring_pass(table, lambda couple: stacks[couple % 2][...], fill, emit, out_rows, width + 2 * reach, wide, hook)

    def place_of(index):
        return lax.div(index, 2), lax.rem(index, 2)

    arrive(0)
    first_layer(0, None)
    begin(0, 0, False)
    arrive(1)
    first_layer(1, lambda: middle(0, 0))
    begin(0, 1, False)
    end(0, 0)

    def layer_step(index, carried):
        layer, batch = place_of(index)
        before = place_of(index - 1)
        reach = FIRST_REACH - 1
        emit = keeper(band(layer, batch), reach)
        inner_layer(layer - 1, batch, middle_tables[layer - 1], channels, reach, emit, lambda: middle(*before))
        begin(layer, batch, True)
        end(*before)
        return carried

    lax.fori_loop(2, 8, layer_step, 0)

    def last_step(batch, carried):
        def emit(column, value):
            result[batch, 0, column : column + 1] = value[0:1]
            result[batch, 1, column : column + 1] = value[1:2]

        inner_layer(3, batch, last_table[...], 8, 0, emit, lambda: pl.when(batch == 0)(lambda: middle(3, 1)))
        pl.when(batch == 0)(lambda: end(3, 1))
        return carried

    lax.fori_loop(0, 2, last_step, 0)
    for batch in range(2):
        save(3, batch).wait()
    for layer in range(4):
        for batch in range(2):
            sums.settle((layer, batch))


def forward(kspace, maps, target, foreground, row_mask, anatomy, first, middle, last, gains, shifts, parts, images):
    micro, coils, _, rows, length = kspace.shape
    wide = padded(length)
    channels = first.shape[2]
    cosine, sine = phases(length)
    fourier = np.zeros((wide, 2, wide))
    fourier[:length, 0, :length] = cosine
    fourier[:length, 1, :length] = sine
    fourier_high, fourier_low = np_high_low(fourier.reshape(wide, 2 * wide))
    inverse = np.stack([np.stack([cosine, sine], 0), np.stack([-sine, cosine], 0)], 0)
    turn = inverse.reshape(2, 2, length, parts, rows).transpose(0, 3, 1, 4, 2).reshape(2, 2 * length, length)
    pick = np.zeros((2, parts, 2, rows, length), np.float32)
    for part in range(2):
        for block in range(parts):
            pick[part, block, part, :, block * rows : (block + 1) * rows] = np.eye(rows)
    pick = jnp.asarray(pick.reshape(2, 2 * length, length).astype(BF16))
    turn_high, turn_low = np_high_low(turn)
    edge = ((0, wide - length), (0, wide - length))
    cosine = jnp.asarray(np.pad(cosine, edge), F32)
    sine = jnp.asarray(np.pad(sine, edge), F32)
    slots = 2 * micro
    lanes = padded(3 * micro * rows)
    shapes = [
        ((micro, 2, rows, wide), F32),
        ((micro, coils, 2 * rows, wide), BF16),
        ((micro, 3, rows, wide), F32),
        ((micro, 2 * wide, 2 * wide), BF16),
        ((3, 3 * channels, 3 * channels), BF16),
        ((3 * channels, 16), BF16),
        ((4, micro, rows + 2 * BACK_REACH, channels, wide), F32),
        ((4, micro, 4, channels, TILE), F32),
        ((4, micro, 8, channels), F32),
        ((micro, 16, (rows + 2 * FIRST_REACH + 2) * wide), BF16),
        ((micro, 2, rows, wide), F32),
    ]
    layers = (4, micro)
    return pl.pallas_call(
        functools.partial(forward_kernel, (micro, coils, rows, length, parts, images)),
        out_shape=[jax.ShapeDtypeStruct(*shape) for shape in shapes],
        in_specs=[anywhere()] * 2 + [in_vmem()] * 16,
        out_specs=[in_vmem()] * 6 + [anywhere()] + [in_vmem()] * 4,
        scratch_shapes=[
            pltpu.VMEM((2, 2, coils, rows, length), F32),
            pltpu.VMEM((slots, parts, 2 * rows, coils * rows), BF16),
            pltpu.VMEM((slots, parts, 2 * rows, coils * rows), BF16),
            pltpu.VMEM((parts, rows, lanes), F32),
            pltpu.VMEM((parts, rows, lanes), F32),
            pltpu.VMEM((2, micro, 2 * REACH, wide), F32),
            pltpu.VMEM((2, micro, 2 * REACH, wide), F32),
            pltpu.VMEM((3 * channels, 16), BF16),
            pltpu.VMEM((3, 3 * channels, 3 * channels), BF16),
            pltpu.VMEM((24, 3 * channels), BF16),
            pltpu.VMEM((1, TILE), F32),
            pltpu.SemaphoreType.DMA((slots, 2)),
            pltpu.SemaphoreType.DMA((slots, parts - 1)),
            pltpu.SemaphoreType.DMA((slots, parts - 1)),
            pltpu.SemaphoreType.DMA((slots,)),
            pltpu.SemaphoreType.DMA((parts - 1,)),
            pltpu.SemaphoreType.DMA((parts - 1,)),
            pltpu.SemaphoreType.DMA((micro, 2)),
            pltpu.SemaphoreType.DMA((micro, 2)),
            pltpu.VMEM((micro, 2, rows + 2 * FIRST_REACH, channels, wide), F32),
            pltpu.VMEM((3 * channels, 2 * wide), BF16),
            pltpu.VMEM((3 * channels, 2 * wide), BF16),
            pltpu.VMEM((channels, TILE), F32),
            pltpu.VMEM((channels, TILE), F32),
            pltpu.VMEM((channels, TILE), F32),
        ]
        + Sums.scratch(layers, parts, images)
        + [pltpu.SemaphoreType.DMA(layers)],
        compiler_params=params(collective_id=1, has_side_effects=True),
        name="forward",
    )(
        kspace, maps, target, foreground, row_mask, anatomy, first, middle, last, turn_high, turn_low, pick, cosine, sine,
        fourier_high, fourier_low, gains, shifts,
    )


def backward_kernel(
    sizes, grad, halo_image, layers, coefs, rows_in, images_in, middle_back, last_back,
    first_sums, middle_sums, last_sums, rows_out,
    upper, lin, stack, thin, inputs, slope, total, along, mix, *refs,
):
    micro, parts, images, length = sizes
    _, _, width, wide = grad.shape
    channels = lin.shape[3]
    pixels = width * length * parts * images
    sums = Sums(parts, images, refs[:6])
    (loaded,) = refs[6:]
    knock(sums.rows + sums.cols)
    ends = Ends(parts)
    clear = lane_mask(length, wide)

    def load(layer, batch):
        return pltpu.make_async_copy(layers.at[layer, batch], lin.at[batch, lax.rem(layer, 2)], loaded.at[layer, batch])

    for layer in (3, 2):
        for batch in range(micro):
            load(layer, batch).start()
    first_sums[...] = jnp.zeros_like(first_sums)
    middle_sums[...] = jnp.zeros_like(middle_sums)
    last_sums[...] = jnp.zeros_like(last_sums)

    def band(layer, batch):
        return upper.at[batch, lax.rem(layer, 2)]

    def begin(layer, batch):
        added = jnp.concatenate([total[...], along[...]], axis=0).T
        added = jnp.sum(added, axis=0, keepdims=True)
        sums.start((layer, batch), 0, padded_rows([added]))

    def middle(layer, batch):
        sums.start((layer, batch), 1, functools.reduce(jnp.add, sums.collect((layer, batch), 0)))

    def end(layer, batch):
        added = functools.reduce(jnp.add, sums.collect((layer, batch), 1))
        shift_sum, gain_sum = added[0:1, :channels], added[0:1, channels:]
        rows = rows_in[layer, batch]
        gain, inverse, offset = rows[0:1], rows[2:3], rows[3:4]
        scale = inverse * gain
        mix[batch, 0] = spread_row(scale)
        mix[batch, 1] = spread_row(-scale * inverse * gain_sum / pixels)
        mix[batch, 2] = spread_row(-scale * (shift_sum + offset * gain_sum) / pixels)
        rows_out[layer, batch] = join_rows([shift_sum, gain_sum], 8)

    def place_of(index):
        return 3 - lax.div(index, 2), lax.rem(index, 2)

    def grad_putter(layer, batch):
        grads, linear = band(layer, batch), lin.at[batch, lax.rem(layer, 2)]
        on_grad, on_layer, base = (repeat_lanes(mix[batch, index], wide) for index in range(3))

        def put(column):
            at = column + BACK_REACH
            upstream = clear(on_grad * grads[at] + on_layer * linear[at] + base)
            put_shifted(stack, ends.clear(upstream, column, width).astype(BF16), at * wide)

        return put

    def add_weights(weight_out, source, reach, around, around_reach, first):
        at = first + around_reach - 1
        columns = [around[:, (at + tap) * wide : (at + tap + GROUP) * wide] for tap in range(3)]
        at = first + reach
        weight_out[...] += dot_nt(source[:, at * wide : (at + GROUP) * wide], jnp.concatenate(columns, axis=0))

    def layer_back(layer, batch, source, reach, table, weight_out, put_grad, hook):
        below = lin.at[batch, lax.rem(layer, 2)]
        out = band(layer, batch)
        scale, offset = repeat_lanes(coefs[layer, batch, 0], wide), repeat_lanes(coefs[layer, batch, 1], wide)
        inverse, centre = repeat_lanes(coefs[layer, batch, 2], wide), repeat_lanes(coefs[layer, batch, 3], wide)

        def fill(couple):
            for place in range(2):
                column = 2 * couple + place - reach - 1
                if put_grad is not None:
                    put_grad(column)
                if not -reach <= column < width + reach:
                    continue
                at = column + BACK_REACH
                half, curve = silu_half(below[at], scale, offset)
                slope[at] = 0.5 * (1.0 + curve) * (1.0 + half * (1.0 - curve))
                if -1 <= column <= width:
                    active = ends.clear(clear(half * curve + half), column, width)
                    inputs[:, (column + 1) * wide : (column + 2) * wide] = active.astype(BF16)

        held = []

        def emit(column, value):
            column = column - reach
            at = column + BACK_REACH
            shaped = clear(value * slope[at])
            out[at] = shaped
            if not 0 <= column < width:
                return
            if column % BLOCK == 0:
                held[:] = [jnp.zeros((channels, TILE), F32), jnp.zeros((channels, TILE), F32)]
            held[0] = held[0] + fold(shaped)
            held[1] = held[1] + fold(shaped * (below[at] * inverse + centre))
            if column == BLOCK - 1:
                total[...], along[...] = held
            elif column % BLOCK == BLOCK - 1:
                total[...] += held[0]
                along[...] += held[1]
            if column % GROUP == GROUP - 1:
                add_weights(weight_out, source, reach + 1, inputs, 1, column + 1 - GROUP)

        ring_pass(
            table,
            lambda couple: source[:, 2 * couple * wide : 2 * (couple + 1) * wide],
            fill,
            emit,
            channels,
            width + 2 * reach,
            wide,
            hook,
        )

    def outer_step(batch, carried):
        put_image(grad.at[batch], halo_image, batch, thin, ends, BACK_REACH + 1)
        pl.when(batch == 0)(lambda: admit(sums.rows + sums.cols))
        load(3, batch).wait()
        hook = lambda: pl.when(batch > 0)(lambda: middle(3, 0))
        layer_back(3, batch, thin, BACK_REACH, last_back[...], last_sums, None, hook)
        begin(3, batch)
        pl.when(batch > 0)(lambda: end(3, 0))
        return carried

    lax.fori_loop(0, 2, outer_step, 0)

    def layer_step(index, carried):
        layer, batch = place_of(index)
        before = place_of(index - 1)
        load(layer, batch).wait()
        layer_back(
            layer,
            batch,
            stack,
            BACK_REACH - 1,
            middle_back[layer],
            middle_sums.at[layer],
            grad_putter(layer + 1, batch),
            lambda: middle(*before),
        )
        pl.when(layer > 0)(lambda: load(layer - 1, batch).start())
        begin(layer, batch)
        end(*before)
        return carried

    lax.fori_loop(2, 8, layer_step, 0)

    def first_step(batch, carried):
        put_grad = grad_putter(0, batch)
        for column in range(width):
            if column == width // 2:
                pl.when(batch == 0)(lambda: middle(0, 1))
            put_grad(column)
            if column % GROUP == GROUP - 1:
                add_weights(first_sums, stack, BACK_REACH, images_in.at[batch], FIRST_REACH + 1, column + 1 - GROUP)
        pl.when(batch == 0)(lambda: end(0, 1))
        return carried

    lax.fori_loop(0, 2, first_step, 0)
    for layer in range(4):
        for batch in range(2):
            sums.settle((layer, batch))


def backward(grad, halo, kept, tables, parts, images, length):
    layers, coefs, rows_in, images_in = kept
    micro, _, width, wide = grad.shape
    channels = layers.shape[3]
    band = (micro, 2, width + 2 * BACK_REACH, channels, wide)
    lanes = (width + 2 * BACK_REACH) * wide
    shapes = [(3 * channels, 48), (3, 3 * channels, 3 * channels), (16, 3 * channels), (4, micro, 8, channels)]
    slots = (4, micro)
    return pl.pallas_call(
        functools.partial(backward_kernel, (micro, parts, images, length)),
        out_shape=[jax.ShapeDtypeStruct(shape, F32) for shape in shapes],
        in_specs=[in_vmem(), in_vmem(), anywhere()] + [in_vmem()] * 5,
        out_specs=[in_vmem()] * 4,
        scratch_shapes=[
            pltpu.VMEM(band, F32),
            pltpu.VMEM(band, F32),
            pltpu.VMEM((3 * channels, lanes), BF16),
            pltpu.VMEM((16, lanes + 2 * wide), BF16),
            pltpu.VMEM((channels, (width + 2) * wide), BF16),
            pltpu.VMEM(band[2:], F32),
            pltpu.VMEM((channels, TILE), F32),
            pltpu.VMEM((channels, TILE), F32),
            pltpu.VMEM((micro, 3, channels, TILE), F32),
        ]
        + Sums.scratch(slots, parts, images)
        + [pltpu.SemaphoreType.DMA(slots)],
        compiler_params=params(collective_id=3, has_side_effects=True),
        name="backward",
    )(grad, halo, layers, coefs, rows_in, images_in, *tables)


def reduce_kernel(parts, images, first_sums, middle_sums, last_sums, scalars, first_grad, middle_grad, last_grad, totals, whole, final, quarter, landed, eighth, landed_rows, send, receive):
    image, me = lax.axis_index("img"), lax.axis_index("row")
    rows, cols = row_peers(parts), image_peers(images)
    knock(rows + cols)
    channels = middle_sums.shape[1] // 3
    taps = [(kr, kw) for kr in range(3) for kw in range(3)]
    pieces = [
        middle_sums[layer, (2 - kr) * channels : (3 - kr) * channels, kw * channels : (kw + 1) * channels]
        for layer in range(3)
        for kr, kw in taps
    ]
    firsts = [first_sums[(2 - kr) * channels : (3 - kr) * channels, 16 * kw + 2 : 16 * kw + 4] for kr, kw in taps]
    pieces.append(join_lanes(firsts, channels))
    for index in range(0, len(pieces), 2):
        at = index // 2 * channels
        whole[at : at + channels] = jnp.concatenate(pieces[index : index + 2], axis=1)
    at = len(pieces) // 2 * channels
    lasts = [last_sums[2 * (2 - kr) : 2 * (3 - kr), kw * channels : (kw + 1) * channels] for kr, kw in taps]
    added = functools.reduce(jnp.add, [scalars[batch] for batch in range(scalars.shape[0])])
    whole[at : at + 24] = jnp.concatenate([join_rows(lasts, 24), join_rows([added[:, :channels]], 24)], axis=1)
    whole[at + 24 :] = jnp.zeros((whole.shape[0] - at - 24, TILE), F32)
    admit(rows + cols)
    big, small = quarter.shape[0], eighth.shape[0]
    images_here, parts_here = len(cols), len(rows)

    def place(index, size):
        return pl.ds(pl.multiple_of(index * size, 8), size)

    sent = []
    for index, peer in enumerate(cols):
        copy = remote(whole.at[place(peer[0], big)], landed.at[index], send.at[index], receive.at[index], peer)
        copy.start()
        sent.append(copy)
    for copy in sent:
        copy.wait_recv()
    total = whole[place(image, big)]
    for index in range(images_here):
        total = total + landed[index]
    quarter[...] = total
    base = images_here
    arrived = []
    for index, peer in enumerate(rows):
        copy = remote(
            quarter.at[place(peer[1], small)], landed_rows.at[index], send.at[base + index], receive.at[base + index], peer
        )
        copy.start()
        arrived.append(copy)
    for copy in arrived:
        copy.wait_recv()
    total = quarter[place(me, small)]
    for index in range(parts_here):
        total = total + landed_rows[index]
    eighth[...] = total
    for copy in sent + arrived:
        copy.wait_send()
    base += parts_here
    returned = []
    mine = pl.ds(pl.multiple_of(image * big + me * small, 8), small)
    for index, peer in enumerate(rows):
        copy = remote(eighth, final.at[mine], send.at[base + index], receive.at[base + index], peer)
        copy.start()
        returned.append(copy)
    final[mine] = total
    for copy in returned:
        copy.wait()
    base += parts_here
    returned = []
    for index, peer in enumerate(cols):
        copy = remote(final.at[place(image, big)], final.at[place(image, big)], send.at[base + index], receive.at[base + index], peer)
        copy.start()
        returned.append(copy)
    for copy in returned:
        copy.wait()
    for index in range(27):
        from_row = index // 2 * channels
        from_lane = index % 2 * channels
        middle_grad[index // 9, index % 9] = final[from_row : from_row + channels, from_lane : from_lane + channels]
    turned = final[13 * channels : 14 * channels, channels:].T
    for tap in range(9):
        first_grad[tap] = turned[2 * tap : 2 * tap + 2]
        last_grad[tap] = final[at + 2 * tap : at + 2 * tap + 2, :channels]
    totals[...] = final[at : at + 8, channels:]


def reduce_all(first_sums, middle_sums, last_sums, scalars, parts, images):
    channels = middle_sums.shape[1] // 3
    unit = 8 * parts * images
    height = -(-(14 * channels + 24) // unit) * unit
    copies = 2 * (parts + images - 2)
    shapes = [(9, 2, channels), (3, 9, channels, channels), (9, 2, channels), (8, channels)]
    return pl.pallas_call(
        functools.partial(reduce_kernel, parts, images),
        out_shape=[jax.ShapeDtypeStruct(shape, F32) for shape in shapes],
        in_specs=[in_vmem()] * 4,
        out_specs=[in_vmem()] * 4,
        scratch_shapes=[
            pltpu.VMEM((height, TILE), F32),
            pltpu.VMEM((height, TILE), F32),
            pltpu.VMEM((height // images, TILE), F32),
            pltpu.VMEM((images - 1, height // images, TILE), F32),
            pltpu.VMEM((height // images // parts, TILE), F32),
            pltpu.VMEM((parts - 1, height // images // parts, TILE), F32),
            pltpu.SemaphoreType.DMA((copies,)),
            pltpu.SemaphoreType.DMA((copies,)),
        ],
        compiler_params=params(collective_id=4, has_side_effects=True),
        name="reduce_all",
    )(first_sums, middle_sums, last_sums, scalars)


def apply_normal(image, maps, normal, diagonal):
    coils, slabs, wide = maps.shape
    rows = slabs // 2
    real, imag = image
    stack, power = [], jnp.zeros((rows, wide), F32)
    for coil in range(coils):
        sense = maps[coil].astype(F32)
        sense_re, sense_im = sense[:rows], sense[rows:]
        power = power + sense_re * sense_re + sense_im * sense_im
        field = [sense_re * real - sense_im * imag, sense_re * imag + sense_im * real]
        stack.append(jnp.concatenate(field, axis=1))
    stack = jnp.concatenate(stack, axis=0).astype(BF16)
    power = diagonal * power
    out_re, out_im = power * real, power * imag
    turned = dot(stack, normal[...])
    for coil in range(coils):
        sense = maps[coil].astype(F32)
        sense_re, sense_im = sense[:rows], sense[rows:]
        field = turned[coil * rows : (coil + 1) * rows]
        field_re, field_im = field[:, :wide], field[:, wide:]
        out_re = out_re + sense_re * field_re + sense_im * field_im
        out_im = out_im + sense_re * field_im - sense_im * field_re
    return out_re, out_im


def pair(ref):
    return ref[0], ref[1]


def put_pair(ref, values):
    ref[0] = values[0]
    ref[1] = values[1]


def blend(*terms):
    return tuple(functools.reduce(jnp.add, [factor * image[part] for factor, image in terms]) for part in range(2))


def inner_of(left, right):
    product = left[0] * right[0] + left[1] * right[1]
    return jnp.sum(jnp.sum(product, axis=1, keepdims=True), axis=0, keepdims=True)


class RowSums:
    def __init__(self, parts, refs):
        self.message, self.held, self.send, self.receive = refs
        self.peers = row_peers(parts)

    def copies(self, slot):
        return [
            remote(
                self.message.at[slot],
                self.held.at[slot + (index,)],
                self.send.at[slot + (index,)],
                self.receive.at[slot + (index,)],
                peer,
            )
            for index, peer in enumerate(self.peers)
        ]

    def start(self, slot, values):
        filler = [jnp.zeros((1, TILE), F32)] * (8 - len(values))
        self.message[slot] = jnp.concatenate([jnp.broadcast_to(value, (1, TILE)) for value in values] + filler, axis=0)
        for copy in self.copies(slot):
            copy.start()

    def finish(self, slot):
        total = self.message[slot]
        for index, copy in enumerate(self.copies(slot)):
            copy.wait_recv()
            total = total + self.held[slot + (index,)]
        return [total[index : index + 1, 0:1] for index in range(8)]

    def settle(self, slot):
        for copy in self.copies(slot):
            copy.wait_send()


def solve_kernel(
    sizes, filled, result, maps, normal, planes, rows_in, row_mask, extra, grad_out, halo, scalars,
    work, edges, send_edge, receive_edge, *refs,
):
    micro, parts, length = sizes
    _, _, rows, wide = filled.shape
    sums = RowSums(parts, refs)
    knock(sums.peers)
    moved = []
    inside = lax.broadcasted_iota(jnp.int32, (rows, wide), 1) < length
    penalty = jnp.exp(jnp.full((1, 1), extra[2], F32))
    inv_count = 1.0 / rows_in[0, 0, 4:5, 0:1]
    diagonals = [jnp.sum(row_mask[batch].astype(F32), axis=1, keepdims=True) / length for batch in range(micro)]
    names = ("denoised", "right", "mapped", "residue", "through", "search", "searched", "slope")

    def at(name, batch):
        return work.at[batch, names.index(name)]

    def get(name, batch):
        return pair(at(name, batch))

    def through_normal(image, batch):
        out = apply_normal(image, maps.at[batch], normal.at[batch], diagonals[batch])
        return blend((1.0, out), (penalty, image))

    for batch in range(micro):
        images = []
        for part in range(2):
            value = filled[batch, part] + result[batch, part] + jnp.full((1, 1), extra[part], F32)
            value = jnp.where(inside, value, 0.0)
            at("denoised", batch)[part] = value
            images.append(filled[batch, part] + penalty * value)
        put_pair(at("right", batch), images)
        mapped = through_normal(images, batch)
        put_pair(at("mapped", batch), mapped)
        if batch == 0:
            admit(sums.peers)
        sums.start((0, batch), [inner_of(images, images), inner_of(images, mapped)])
    ones, twos = [], []
    for batch in range(micro):
        ones.append(sums.finish((0, batch)))
        start, image = get("right", batch), get("mapped", batch)
        left_over = blend((1.0, start), (-ones[batch][0] / ones[batch][1], image))
        put_pair(at("residue", batch), left_over)
        mapped = through_normal(left_over, batch)
        put_pair(at("through", batch), mapped)
        sums.start(
            (1, batch),
            [
                inner_of(left_over, left_over),
                inner_of(left_over, mapped),
                inner_of(left_over, image),
                inner_of(start, mapped),
            ],
        )
    kept = []
    for batch in range(micro):
        twos.append(sums.finish((1, batch)))
        norm_0, curve_0 = ones[batch][:2]
        norm_1 = twos[batch][0]
        factor = norm_1 / norm_0
        curve_1 = twos[batch][1] + factor * (twos[batch][2] + twos[batch][3]) + factor * factor * curve_0
        start, image = get("right", batch), get("mapped", batch)
        direction = blend((1.0, get("residue", batch)), (factor, start))
        image_1 = blend((1.0, get("through", batch)), (factor, image))
        put_pair(at("searched", batch), image_1)
        state = blend((norm_0 / curve_0, start), (norm_1 / curve_1, direction))
        weight = planes[batch, 2]
        difference = [state[part] - planes[batch, part] for part in range(2)]
        grad = [inv_count * 2.0 * weight * difference[part] for part in range(2)]
        put_pair(at("slope", batch), grad)
        masked = [weight * difference[part] for part in range(2)]
        sums.start(
            (2, batch),
            [
                inner_of(grad, direction),
                inner_of(grad, start),
                inner_of(grad, image),
                inner_of(image_1, start),
                inner_of(image_1, image),
            ],
        )
        kept.append((norm_0, curve_0, norm_1, curve_1, factor, inner_of(direction, direction), inner_of(masked, difference)))
    for batch in range(micro):
        grad_search, grad_start, grad_image, cross_start, cross_image = sums.finish((2, batch))[:5]
        norm_0, curve_0, norm_1, curve_1, factor, own_search, own_loss = kept[batch]
        step_0, step_1 = norm_0 / curve_0, norm_1 / curve_1
        start, image, left_over = get("right", batch), get("mapped", batch), get("residue", batch)
        image_1, grad = get("searched", batch), get("slope", batch)
        residue_image = twos[batch][2]
        curve_grad_1 = -grad_search * norm_1 / (curve_1 * curve_1)
        norm_grad_1 = grad_search / curve_1
        search_grad = blend((step_1, grad), (2.0 * curve_grad_1, image_1))
        factor_grad = step_1 * grad_start + 2.0 * curve_grad_1 * cross_start
        joint = step_1 * grad_image + 2.0 * curve_grad_1 * cross_image
        norm_total = norm_grad_1 + factor_grad / norm_0
        residue_full = blend((1.0, search_grad), (2.0 * norm_total, left_over))
        step_grad = grad_start - (joint + 2.0 * norm_total * residue_image)
        curve_grad_0 = -step_grad * norm_0 / (curve_0 * curve_0)
        mapped_grad = blend((-step_0, residue_full), (curve_grad_0, start))
        through = through_normal(mapped_grad, batch)
        norm_grad_0 = -factor_grad * norm_1 / (norm_0 * norm_0) + step_grad / curve_0
        right_grad = blend(
            (1.0, residue_full),
            (factor, search_grad),
            (step_0, grad),
            (curve_grad_0, image),
            (1.0, through),
            (2.0 * norm_grad_0, start),
        )
        penalty_part = (
            curve_grad_1 * own_search + inner_of(mapped_grad, start) + inner_of(right_grad, get("denoised", batch))
        )
        grad_pair = [penalty * right_grad[part] for part in range(2)]
        put_pair(grad_out.at[batch], grad_pair)
        put_edges(edges.at[:, batch], *grad_pair)
        for copy in image_halo(parts, batch, edges, halo, send_edge, receive_edge):
            copy.start()
            moved.append(copy)
        offsets = [jnp.sum(jnp.sum(grad_pair[part], axis=1, keepdims=True), axis=0, keepdims=True) for part in range(2)]
        values = [offsets[0], offsets[1], penalty * penalty_part, own_loss]
        scalars[batch] = join_rows([jnp.broadcast_to(value, (1, TILE)) for value in values], 8)
    for stage in range(3):
        for batch in range(micro):
            sums.settle((stage, batch))
    for copy in moved:
        copy.wait()


def solve_all(filled, result, maps, normal, planes, rows_in, row_mask, extra, parts, length):
    micro, _, rows, wide = filled.shape
    shapes = [(micro, 2, rows, wide), (2, micro, 2 * REACH, wide), (micro, 8, TILE)]
    slots = (3, micro)
    return pl.pallas_call(
        functools.partial(solve_kernel, (micro, parts, length)),
        out_shape=[jax.ShapeDtypeStruct(shape, F32) for shape in shapes],
        in_specs=[in_vmem()] * 7 + [pl.BlockSpec(memory_space=pltpu.SMEM)],
        out_specs=[in_vmem()] * 3,
        scratch_shapes=[
            pltpu.VMEM((micro, 8, 2, rows, wide), F32),
            pltpu.VMEM((2, micro, 2 * REACH, wide), F32),
            pltpu.SemaphoreType.DMA((micro, 2)),
            pltpu.SemaphoreType.DMA((micro, 2)),
            pltpu.VMEM(slots + (8, TILE), F32),
            pltpu.VMEM(slots + (parts - 1, 8, TILE), F32),
            pltpu.SemaphoreType.DMA(slots + (parts - 1,)),
            pltpu.SemaphoreType.DMA(slots + (parts - 1,)),
        ],
        compiler_params=params(collective_id=5, has_side_effects=True),
        name="solve_all",
    )(filled, result, maps, normal, planes, rows_in, row_mask, extra)


def update_kernel(weights, means, squares, grads, rows_back, totals, rows_in, outs):
    first_grad, middle_grad, last_grad = grads
    affine = []
    for row in (1, 0):
        rows = [functools.reduce(jnp.add, [rows_back[layer, batch, row : row + 1] for batch in range(rows_back.shape[1])]) for layer in range(4)]
        affine.append(jnp.concatenate(rows, axis=0))
    extra = join_lanes([totals[index : index + 1, 0:1] for index in range(3)], 3)

    def put(group, at, gradient, refs):
        results = adamw(weights[group][at], gradient, means[group][at], squares[group][at], LEARN_RATES[group])
        for ref, value in zip(refs, results + (results[0].astype(BF16),)):
            ref[at] = value

    everything = (slice(None), slice(None))
    for tap in range(9):
        put(0, tap, first_grad[tap], outs[0:4])
        put(2, tap, last_grad[tap], outs[8:12])
        for layer in range(3):
            put(1, (layer, tap), middle_grad[layer, tap], outs[4:8])
    put(3, everything, affine[0], outs[12:15])
    put(4, everything, affine[1], outs[15:18])
    put(5, everything, extra, outs[18:21])
    outs[21][...] = totals[3:4, 0:1]
    outs[22][...] = rows_in[0, 0, 4:5, 0:1].astype(jnp.int32)


def update(weights, means, squares, grads, rows_back, totals, rows_in):
    shapes = []
    for group, weight in enumerate(weights):
        shapes += [jax.ShapeDtypeStruct(weight.shape, F32)] * 3
        if group < 3:
            shapes.append(jax.ShapeDtypeStruct(weight.shape, BF16))
    shapes += [jax.ShapeDtypeStruct((1, 1), F32), jax.ShapeDtypeStruct((1, 1), jnp.int32)]

    def kernel(*refs):
        update_kernel(refs[0:6], refs[6:12], refs[12:18], refs[18:21], refs[21], refs[22], refs[23], refs[24:])

    return pl.pallas_call(
        kernel,
        out_shape=shapes,
        in_specs=[in_vmem()] * 24,
        out_specs=[in_vmem()] * len(shapes),
        compiler_params=params(),
        name="update",
    )(*weights, *means, *squares, *grads, rows_back, totals, rows_in)


def fast_step(arrays, moments):
    (
        kspace, coil_maps, target, row_mask, foreground, anatomy, first_weight, middle_weight, last_weight, norm_gains, norm_shifts, extra_params,
    ) = arrays
    length = kspace.shape[-1]
    parts, images = lax.axis_size("row"), lax.axis_size("img")
    filled, maps, planes, normal, middle_back, last_back, layers, coefs, rows_out, images_out, result = forward(
        kspace[:, 0], coil_maps[:, 0], target[:, 0], foreground[:, 0], row_mask, anatomy.transpose(1, 0),
        first_weight.transpose(0, 2, 1), middle_weight, last_weight, norm_gains, norm_shifts, parts, images,
    )
    grad, halo, scalars = solve_all(
        filled, result, maps, normal, planes, rows_out, row_mask, extra_params, parts, length
    )
    first_sums, middle_sums, last_sums, rows_back = backward(
        grad, halo, (layers, coefs, rows_out, images_out), (middle_back, last_back), parts, images, length
    )
    *grads, totals = reduce_all(first_sums, middle_sums, last_sums, scalars, parts, images)

    def turn(group):
        first, middle, last, gains, shifts, extra = group
        return [first.transpose(0, 2, 1), middle, last, gains, shifts, extra.reshape(1, 3)]

    weights = (first_weight, middle_weight, last_weight, norm_gains, norm_shifts, extra_params)
    means, squares = zip(*moments)
    outs = list(update(turn(weights), turn(means), turn(squares), grads, rows_back, totals, rows_out))
    outs[0:4] = [value.transpose(0, 2, 1) for value in outs[0:4]]
    outs[18:21] = [value.reshape(3) for value in outs[18:21]]
    return tuple(outs[:21]) + (outs[21].reshape(()), outs[22].reshape(()))


def local(
    kspace,
    coil_maps,
    target,
    row_mask,
    foreground,
    anatomy,
    first_weight,
    middle_weight,
    last_weight,
    norm_gains,
    norm_shifts,
    extra_params,
    first_mean,
    first_square,
    middle_mean,
    middle_square,
    last_mean,
    last_square,
    gains_mean,
    gains_square,
    shifts_mean,
    shifts_square,
    extra_mean,
    extra_square,
):
    arrays = (
        kspace, coil_maps, target, row_mask, foreground, anatomy, first_weight, middle_weight, last_weight, norm_gains, norm_shifts, extra_params,
    )
    moments = (
        (first_mean, first_square),
        (middle_mean, middle_square),
        (last_mean, last_square),
        (gains_mean, gains_square),
        (shifts_mean, shifts_square),
        (extra_mean, extra_square),
    )
    if fits(kspace, first_weight, lax.axis_size("row")):
        return fast_step(arrays, moments)
    totals, pixel_total = general_local(arrays)
    params = (first_weight, middle_weight, last_weight, norm_gains, norm_shifts, extra_params)
    results = []
    for group in range(6):
        updated, first_new, second_new = adamw(
            params[group], totals[group], moments[group][0], moments[group][1], LEARN_RATES[group]
        )
        results.extend([updated, first_new, second_new])
        if group < 3:
            results.append(updated.astype(jnp.bfloat16))
    return tuple(results) + (totals[6], pixel_total.astype(jnp.int32))


def solution(mesh):
    in_specs = (
        P(None, "img", None, None, "row", None),
        P(None, "img", None, None, "row", None),
        P(None, "img", None, "row", None),
        P(None, "img", None),
        P(None, "img", "row", None),
        P(None, "img"),
        P(),
        P(),
        P(),
        P(),
        P(),
        P(),
        P(),
        P(),
        P(),
        P(),
        P(),
        P(),
        P(),
        P(),
        P(),
        P(),
        P(),
        P(),
    )
    out_specs = (
        P(),
        P(),
        P(),
        P(),
        P(),
        P(),
        P(),
        P(),
        P(),
        P(),
        P(),
        P(),
        P(),
        P(),
        P(),
        P(),
        P(),
        P(),
        P(),
        P(),
        P(),
        P(),
        P(),
    )
    return jax.shard_map(local, mesh=mesh, in_specs=in_specs, out_specs=out_specs, check_vma=False)
```

profile of v0, /device:TPU:0, one launch (start us, length us, event | category | flops | bytes accessed | tf_op | source)
XLA Modules:
  0.0 269.8 jit_solution(9528373534576715112)
XLA Ops:
  0.7 146.2 %forward.1 = (f32[2,2,40,384]{3,2,1,0:T(8,128)}, bf16[2,16,80,384]{3,2,1,0:T(8,128)(2,1)}, f32[2,3,40,384]{3,2,1,0:T(8,128)}, bf16[2,768,768]{2,1,0:T(8,128)(2,1...) custom-call(f32[2,16,2,40,320]{4,3,2,1,0:T(8,128)} %bitcast.20, ...), custom_call_target="tpu_custom_call" | custom-call | tf_op jit(solution)/shard_map/forward/pallas_call | solution.py:1055
  146.8 24.1 %solve_all.1 = (f32[2,2,40,384]{3,2,1,0:T(8,128)}, f32[2,2,16,384]{3,2,1,0:T(8,128)}, f32[2,8,128]{2,1,0:T(8,128)}) custom-call(f32[2,2,40,384]{3,2,1,0:T(8,128)} %get-tuple-element.68.filled, f32[2,2,40,384]{3,2,1,0:T(8,128)} %get-tuple-element.69.result, bf16[2,16,80,384]{3,2,1,0:T(8,128)(2,1)} %get-tuple-element.70.maps, ...), custom_call_target="tpu_custom_call" | custom-call | tf_op jit(solution)/shard_map/solve_all/pallas_call | solution.py:1618
  170.9 66.2 %backward.1 = (f32[192,48]{1,0:T(8,128)}, f32[3,192,192]{2,1,0:T(8,128)}, f32[16,192]{1,0:T(8,128)}, f32[4,2,8,64]{3,2,1,0:T(8,128)}) custom-call(f32[2,2,40,384]{3,2,1,0:T(8,128)} %get-tuple-element.74.grad, f32[2,2,16,384]{3,2,1,0:T(8,128)} %get-tuple-element.75.halo_image, f32[4,2,46,64,384]{4,3,2,1,0:T(8,128)} %get-tuple-element.76.layers, ...), custom_call_target="tpu_custom_call" | custom-call | tf_op jit(solution)/shard_map/backward/pallas_call | solution.py:1274
  237.1 28.1 %reduce_all.1 = (f32[9,2,64]{2,1,0:T(2,128)}, f32[3,9,64,64]{3,2,1,0:T(8,128)}, f32[9,2,64]{2,1,0:T(2,128)}, f32[8,64]{1,0:T(8,128)}) custom-call(f32[192,48]{1,0:T(8,128)} %get-tuple-element.81.first_sums, f32[3,192,192]{2,1,0:T(8,128)} %get-tuple-element.82.middle_sums, f32[16,192]{1,0:T(8,128)} %get-tuple-element.83.last_sums, ...), custom_call_target="tpu_custom_call" | custom-call | tf_op jit(solution)/shard_map/reduce_all/pallas_call | solution.py:1387
  265.2 4.4 %update.1 = (f32[9,2,64]{2,1,0:T(2,128)}, f32[9,2,64]{2,1,0:T(2,128)}, f32[9,2,64]{2,1,0:T(2,128)}, bf16[9,2,64]{2,1,0:T(2,128)(2,1)}, f32[3,9,64,64]{3,2,1,0:T(...) custom-call(f32[9,2,64]{2,1,0:T(2,128)} %bitcast.25, ...), custom_call_target="tpu_custom_call" | custom-call | tf_op jit(solution)/shard_map/update/pallas_call | solution.py:1675
where the time goes:
time: 274 us; the launch traced here: 270 us
  Pallas kernels  269 us (98%)
    pallas_call x1, Pallas kernels, forward(): pl.pallas_call(functools.partial(forward_kernel, (micro, coils, rows, len...  146 us
    pallas_call x1, Pallas kernels, backward(): pl.pallas_call(functools.partial(backward_kernel, (micro, parts, images,...  66.2 us
    pallas_call x1, Pallas kernels, reduce_all(): pl.pallas_call(functools.partial(reduce_kernel, parts, images), out_shape...  28.1 us
    pallas_call x1, Pallas kernels, solve_all(): pl.pallas_call(functools.partial(solve_kernel, (micro, parts, length)), o...  24.1 us

commit v1 on v0

--- a/solution.py
+++ b/solution.py
@@ -366,7 +366,8 @@
 BACK_REACH = 3
 FIRST_REACH = 6
 GROUP = 4
-HOOK_PART = 4
+FORWARD_HOOK = 4
+BACK_HOOK = 5
 REACH = 8
 VMEM_BYTES = 58 * 1024 * 1024
 
@@ -551,7 +552,10 @@
 
     for index in range(len(slots) - 1):
         send_slot(index)
-    flats = exchange_planes(sizes, target, foreground, pick, counted, flat, landed, send_flat, receive_flat, me, peers)
+    put_flat = functools.partial(
+        exchange_planes, sizes, target, foreground, pick, counted, flat, landed, send_flat, receive_flat, me, peers
+    )
+    flats = []
     for batch in range(micro):
         chosen = join_lanes([row_mask[batch].astype(F32)], wide)
         cos_on, sin_on = cosine[...] * chosen, sine[...] * chosen
@@ -588,17 +592,20 @@
             copy.start()
         if batch == 0:
             send_slot(len(slots) - 1)
-            for copy in flats:
-                copy.wait()
-            for image_batch in range(micro):
-                for plane in range(3):
-                    at = (3 * image_batch + plane) * rows
-                    pieces = [landed[block, :, at : at + rows] for block in range(parts)]
-                    planes[image_batch, plane] = join_lanes(pieces, wide)
+            flats.extend(put_flat())
         for copy in moved:
             copy.wait()
 
-    return arrive
+    def finish():
+        for copy in flats:
+            copy.wait()
+        for batch in range(micro):
+            for plane in range(3):
+                at = (3 * batch + plane) * rows
+                pieces = [landed[block, :, at : at + rows] for block in range(parts)]
+                planes[batch, plane] = join_lanes(pieces, wide)
+
+    return arrive, finish
 
 
 def exchange_planes(
@@ -804,7 +811,7 @@
         return values
 
 
-def ring_pass(table, take, fill, emit, out_rows, width, wide, hook):
+def ring_pass(table, take, fill, emit, out_rows, width, wide, hook, hook_at):
     fill(0)
     fill(1)
     product = dot(table, take(0))
@@ -812,7 +819,7 @@
     newer = product[0:out_rows, wide:]
     last = width // 2
     for couple in range(1, last + 1):
-        if hook is not None and couple == last * HOOK_PART // 8:
+        if hook is not None and couple == last * hook_at // 8:
             hook()
         product = dot(table, take(couple))
         if couple < last:
@@ -873,7 +880,7 @@
     ends = Ends(parts)
     clear = lane_mask(length, wide)
     knock(sums.rows + sums.cols)
-    arrive = start_exchange(
+    arrive, finish = start_exchange(
         (micro, coils, rows, length, parts), lambda: admit(sums.rows + sums.cols),
         kspace, maps, target, foreground, row_mask, anatomy, first, middle_weight, last, turn_high, turn_low, pick, cosine, sine,
         fourier_high, fourier_low,
@@ -961,6 +968,7 @@
             width + 2 * FIRST_REACH,
             wide,
             hook,
+            FORWARD_HOOK,
         )
 
     def inner_layer(layer, batch, table, out_rows, reach, emit, hook):
@@ -974,7 +982,7 @@
                 active = ends.clear(clear(half * curve + half), column, width)
                 put_shifted(stacks[couple % 2], active.astype(BF16), place * wide)
 
-        ring_pass(table, lambda couple: stacks[couple % 2][...], fill, emit, out_rows, width + 2 * reach, wide, hook)
+        ring_pass(table, lambda couple: stacks[couple % 2][...], fill, emit, out_rows, width + 2 * reach, wide, hook, FORWARD_HOOK)
 
     def place_of(index):
         return lax.div(index, 2), lax.rem(index, 2)
@@ -1009,6 +1017,7 @@
         return carried
 
     lax.fori_loop(0, 2, last_step, 0)
+    finish()
     for batch in range(2):
         save(3, batch).wait()
     for layer in range(4):
@@ -1211,6 +1220,7 @@
             width + 2 * reach,
             wide,
             hook,
+            BACK_HOOK,
         )
 
     def outer_step(batch, carried):

time: 274 us -> 271 us (0.989)
  Pallas kernels: 269 us -> 266 us
where the time goes in v1:
time: 271 us; the launch traced here: 267 us
  Pallas kernels  266 us (98%)
    pallas_call x1, Pallas kernels, forward(): pl.pallas_call(functools.partial(forward_kernel, (micro, coils, rows, len...  144 us
    pallas_call x1, Pallas kernels, backward(): pl.pallas_call(functools.partial(backward_kernel, (micro, parts, images,...  65.2 us
    pallas_call x1, Pallas kernels, reduce_all(): pl.pallas_call(functools.partial(reduce_kernel, parts, images), out_shape...  28.2 us
    pallas_call x1, Pallas kernels, solve_all(): pl.pallas_call(functools.partial(solve_kernel, (micro, parts, length)), o...  24.1 us

profile of v1, /device:TPU:0, one launch (start us, length us, event | category | flops | bytes accessed | tf_op | source)
XLA Modules:
  0.0 266.6 jit_solution(2782982872802830819)
XLA Ops:
  0.7 143.9 %forward.1 = (f32[2,2,40,384]{3,2,1,0:T(8,128)}, bf16[2,16,80,384]{3,2,1,0:T(8,128)(2,1)}, f32[2,3,40,384]{3,2,1,0:T(8,128)}, bf16[2,768,768]{2,1,0:T(8,128)(2,1...) custom-call(f32[2,16,2,40,320]{4,3,2,1,0:T(8,128)} %bitcast.20, ...), custom_call_target="tpu_custom_call" | custom-call | tf_op jit(solution)/shard_map/forward/pallas_call | solution.py:1064
  144.5 24.1 %solve_all.1 = (f32[2,2,40,384]{3,2,1,0:T(8,128)}, f32[2,2,16,384]{3,2,1,0:T(8,128)}, f32[2,8,128]{2,1,0:T(8,128)}) custom-call(f32[2,2,40,384]{3,2,1,0:T(8,128)} %get-tuple-element.68.filled, f32[2,2,40,384]{3,2,1,0:T(8,128)} %get-tuple-element.69.result, bf16[2,16,80,384]{3,2,1,0:T(8,128)(2,1)} %get-tuple-element.70.maps, ...), custom_call_target="tpu_custom_call" | custom-call | tf_op jit(solution)/shard_map/solve_all/pallas_call | solution.py:1628
  168.6 65.2 %backward.1 = (f32[192,48]{1,0:T(8,128)}, f32[3,192,192]{2,1,0:T(8,128)}, f32[16,192]{1,0:T(8,128)}, f32[4,2,8,64]{3,2,1,0:T(8,128)}) custom-call(f32[2,2,40,384]{3,2,1,0:T(8,128)} %get-tuple-element.74.grad, f32[2,2,16,384]{3,2,1,0:T(8,128)} %get-tuple-element.75.halo_image, f32[4,2,46,64,384]{4,3,2,1,0:T(8,128)} %get-tuple-element.76.layers, ...), custom_call_target="tpu_custom_call" | custom-call | tf_op jit(solution)/shard_map/backward/pallas_call | solution.py:1284
  233.8 28.2 %reduce_all.1 = (f32[9,2,64]{2,1,0:T(2,128)}, f32[3,9,64,64]{3,2,1,0:T(8,128)}, f32[9,2,64]{2,1,0:T(2,128)}, f32[8,64]{1,0:T(8,128)}) custom-call(f32[192,48]{1,0:T(8,128)} %get-tuple-element.81.first_sums, f32[3,192,192]{2,1,0:T(8,128)} %get-tuple-element.82.middle_sums, f32[16,192]{1,0:T(8,128)} %get-tuple-element.83.last_sums, ...), custom_call_target="tpu_custom_call" | custom-call | tf_op jit(solution)/shard_map/reduce_all/pallas_call | solution.py:1397
  262.0 4.4 %update.1 = (f32[9,2,64]{2,1,0:T(2,128)}, f32[9,2,64]{2,1,0:T(2,128)}, f32[9,2,64]{2,1,0:T(2,128)}, bf16[9,2,64]{2,1,0:T(2,128)(2,1)}, f32[3,9,64,64]{3,2,1,0:T(...) custom-call(f32[9,2,64]{2,1,0:T(2,128)} %bitcast.25, ...), custom_call_target="tpu_custom_call" | custom-call | tf_op jit(solution)/shard_map/update/pallas_call | solution.py:1685

commit v2 on v1

--- a/solution.py
+++ b/solution.py
@@ -495,7 +495,7 @@
 
 
 def start_exchange(
-    sizes, meet, kspace, maps, target, foreground, row_mask, anatomy, first, middle, last, turn_high, turn_low, pick, cosine, sine,
+    sizes, meet, tables, kspace, maps, target, foreground, row_mask, anatomy, first, middle, last, turn_high, turn_low, pick, cosine, sine,
     fourier_high, fourier_low,
     filled, maps_out, halo, planes, normal, first_table, middle_tables, last_table, middle_back, last_back, counted,
     fields, staged, spread, flat, landed, edges, loaded, send, receive, own, send_flat, receive_flat, send_edge, receive_edge,
@@ -516,6 +516,8 @@
                 loads[index, part].start()
 
     load_field(0)
+    for copy in tables:
+        copy.start()
     load_field(1)
     arrivals = [[] for _ in range(micro)]
     slabs = 2 * rows
@@ -552,6 +554,9 @@
 
     for index in range(len(slots) - 1):
         send_slot(index)
+        if index == 0:
+            for copy in tables:
+                copy.wait()
     put_flat = functools.partial(
         exchange_planes, sizes, target, foreground, pick, counted, flat, landed, send_flat, receive_flat, me, peers
     )
@@ -867,6 +872,7 @@
     filled, maps_out, planes, normal, middle_back, last_back, layers, coefs, rows_out, images_out, result,
     fields, staged, spread, flat, landed, edges, halo_image, first_table, middle_tables, last_table, counted,
     loaded, send, receive, own, send_flat, receive_flat, send_edge, receive_edge,
+    tables_here, tables_loaded,
     lin, even, odd, pivot, total, square, *refs,
 ):
     micro, coils, rows, length, parts, images = sizes
@@ -880,8 +886,15 @@
     ends = Ends(parts)
     clear = lane_mask(length, wide)
     knock(sums.rows + sums.cols)
+    tables = [
+        pltpu.make_async_copy(source, target, tables_loaded.at[index])
+        for index, (source, target) in enumerate(
+            zip((turn_high, turn_low, cosine, sine, fourier_high, fourier_low), tables_here)
+        )
+    ]
+    turn_high, turn_low, cosine, sine, fourier_high, fourier_low = tables_here
     arrive, finish = start_exchange(
-        (micro, coils, rows, length, parts), lambda: admit(sums.rows + sums.cols),
+        (micro, coils, rows, length, parts), lambda: admit(sums.rows + sums.cols), tables,
         kspace, maps, target, foreground, row_mask, anatomy, first, middle_weight, last, turn_high, turn_low, pick, cosine, sine,
         fourier_high, fourier_low,
         filled, maps_out, halo_image, planes, normal, first_table, middle_tables, last_table, middle_back, last_back, counted,
@@ -1064,7 +1077,7 @@
     return pl.pallas_call(
         functools.partial(forward_kernel, (micro, coils, rows, length, parts, images)),
         out_shape=[jax.ShapeDtypeStruct(*shape) for shape in shapes],
-        in_specs=[anywhere()] * 2 + [in_vmem()] * 16,
+        in_specs=[anywhere()] * 2 + [in_vmem()] * 7 + [anywhere()] * 2 + [in_vmem()] + [anywhere()] * 4 + [in_vmem()] * 2,
         out_specs=[in_vmem()] * 6 + [anywhere()] + [in_vmem()] * 4,
         scratch_shapes=[
             pltpu.VMEM((2, 2, coils, rows, length), F32),
@@ -1086,6 +1099,8 @@
             pltpu.SemaphoreType.DMA((parts - 1,)),
             pltpu.SemaphoreType.DMA((micro, 2)),
             pltpu.SemaphoreType.DMA((micro, 2)),
+            [pltpu.VMEM(t.shape, t.dtype) for t in (turn_high, turn_low, cosine, sine, fourier_high, fourier_low)],
+            pltpu.SemaphoreType.DMA((6,)),
             pltpu.VMEM((micro, 2, rows + 2 * FIRST_REACH, channels, wide), F32),
             pltpu.VMEM((3 * channels, 2 * wide), BF16),
             pltpu.VMEM((3 * channels, 2 * wide), BF16),

time: 271 us -> 270 us (level)
  no operation moved by 1% of the time
where the time goes in v2:
time: 270 us; the launch traced here: 266 us
  Pallas kernels  265 us (98%)
    pallas_call x1, Pallas kernels, forward(): pl.pallas_call(functools.partial(forward_kernel, (micro, coils, rows, len...  143 us
    pallas_call x1, Pallas kernels, backward(): pl.pallas_call(functools.partial(backward_kernel, (micro, parts, images,...  65.2 us
    pallas_call x1, Pallas kernels, reduce_all(): pl.pallas_call(functools.partial(reduce_kernel, parts, images), out_shape...  28.2 us
    pallas_call x1, Pallas kernels, solve_all(): pl.pallas_call(functools.partial(solve_kernel, (micro, parts, length)), o...  24.1 us

profile of v2, /device:TPU:0, one launch (start us, length us, event | category | flops | bytes accessed | tf_op | source)
XLA Modules:
  0.0 266.1 jit_solution(10122583597847900798)
XLA Ops:
  0.7 143.4 %forward.1 = (f32[2,2,40,384]{3,2,1,0:T(8,128)}, bf16[2,16,80,384]{3,2,1,0:T(8,128)(2,1)}, f32[2,3,40,384]{3,2,1,0:T(8,128)}, bf16[2,768,768]{2,1,0:T(8,128)(2,1...) custom-call(f32[2,16,2,40,320]{4,3,2,1,0:T(8,128)} %bitcast.20, ...), custom_call_target="tpu_custom_call" | custom-call | tf_op jit(solution)/shard_map/forward/pallas_call | solution.py:1077
  144.0 24.1 %solve_all.1 = (f32[2,2,40,384]{3,2,1,0:T(8,128)}, f32[2,2,16,384]{3,2,1,0:T(8,128)}, f32[2,8,128]{2,1,0:T(8,128)}) custom-call(f32[2,2,40,384]{3,2,1,0:T(8,128)} %get-tuple-element.68.filled, f32[2,2,40,384]{3,2,1,0:T(8,128)} %get-tuple-element.69.result, bf16[2,16,80,384]{3,2,1,0:T(8,128)(2,1)} %get-tuple-element.70.maps, ...), custom_call_target="tpu_custom_call" | custom-call | tf_op jit(solution)/shard_map/solve_all/pallas_call | solution.py:1643
  168.2 65.2 %backward.1 = (f32[192,48]{1,0:T(8,128)}, f32[3,192,192]{2,1,0:T(8,128)}, f32[16,192]{1,0:T(8,128)}, f32[4,2,8,64]{3,2,1,0:T(8,128)}) custom-call(f32[2,2,40,384]{3,2,1,0:T(8,128)} %get-tuple-element.74.grad, f32[2,2,16,384]{3,2,1,0:T(8,128)} %get-tuple-element.75.halo_image, f32[4,2,46,64,384]{4,3,2,1,0:T(8,128)} %get-tuple-element.76.layers, ...), custom_call_target="tpu_custom_call" | custom-call | tf_op jit(solution)/shard_map/backward/pallas_call | solution.py:1299
  233.3 28.2 %reduce_all.1 = (f32[9,2,64]{2,1,0:T(2,128)}, f32[3,9,64,64]{3,2,1,0:T(8,128)}, f32[9,2,64]{2,1,0:T(2,128)}, f32[8,64]{1,0:T(8,128)}) custom-call(f32[192,48]{1,0:T(8,128)} %get-tuple-element.81.first_sums, f32[3,192,192]{2,1,0:T(8,128)} %get-tuple-element.82.middle_sums, f32[16,192]{1,0:T(8,128)} %get-tuple-element.83.last_sums, ...), custom_call_target="tpu_custom_call" | custom-call | tf_op jit(solution)/shard_map/reduce_all/pallas_call | solution.py:1412
  261.5 4.4 %update.1 = (f32[9,2,64]{2,1,0:T(2,128)}, f32[9,2,64]{2,1,0:T(2,128)}, f32[9,2,64]{2,1,0:T(2,128)}, bf16[9,2,64]{2,1,0:T(2,128)(2,1)}, f32[3,9,64,64]{3,2,1,0:T(...) custom-call(f32[9,2,64]{2,1,0:T(2,128)} %bitcast.25, ...), custom_call_target="tpu_custom_call" | custom-call | tf_op jit(solution)/shard_map/update/pallas_call | solution.py:1700
